TPU v7x, 512 devices: a whole 4x8x8 slice. The times are simulated.
512 devices in a mesh: seg: 64 (over x, z, core), tp: 8 (over y).
Axes of the slice: x: 4, y: 8, z: 8, core: 2. Of those that a mesh axis runs over, the one named last changes fastest.
Arguments:
- natural_logged_absorbance: float32 [786432], P('seg'), may hold values from -4 to 4
- lower_state_level: float32 [786432], P('seg'), may hold values from 0 to 3000
- subgrid_shift_ratio: float32 [786432], P('seg'), may hold values from 0 to 1
- local_grid_slot: int32 [786432], P('seg'), may hold values from 0 to 2046
- broadening_class: int32 [786432], P('seg'), may hold values from 0 to 15
- tallies_per_shard: int32 [64, 64], replicated, may hold values from 0 to 768, as said below
- heat_levels: float32 [8], P('tp'), may hold values from 600 to 1200
- sum_over_states_ratio: float32 [8], P('tp'), may hold values from 0.5 to 2
- shape_kernels: float32 [8, 16, 256], P('tp'), may hold values from 0 to 0.00390625
Outputs:
- opacity: float32 [8, 131072], P('tp', 'seg')
Inputs may be any that keep to these rules, and one draw needn't show every extreme that they name: `tallies_per_shard`: each row of counts sums to 12288; one segment, the same for every shard, receives exactly 768 lines from every shard, and no entry exceeds 768.
All inputs are finite; a program needn't handle non-finite values.
Results may differ from a plain program's by a relative error of at most 0.0003.
Values sent between devices are 32-bit elements; how exact they have to be, the bound alone decides.
A program may use at most 64 MiB of HBM per device.

v0:
```python
import math

import jax
import jax.numpy as jnp
from jax import lax
from jax.sharding import PartitionSpec as P

G = 2048
NW = 16


planck_hc_over_boltzmann = 1.4388
baseline_heat_level = 900.0


def extended(cells, sides, width):
    for axis, dim in sides:
        count = lax.axis_size(axis)
        ends = count - 1
        head = lax.slice_in_dim(cells, 0, width, axis=dim)
        tail = lax.slice_in_dim(cells, cells.shape[dim] - width, cells.shape[dim], axis=dim)
        cells = jnp.concatenate(
            [
                lax.ppermute(tail, axis, [(i, (i + 1) % count) for i in range(ends)]),
                cells,
                lax.ppermute(head, axis, [((i + 1) % count, i) for i in range(ends)]),
            ],
            axis=dim,
        )
    return cells


def dft_tables():
    inner = jnp.arange(256, dtype=jnp.int32)
    freqs = jnp.arange(512, dtype=jnp.int32)
    angle = 2.0 * math.pi / 512.0 * (inner[:, None] * freqs[None, :] % 512).astype(jnp.float32)
    forward = jnp.concatenate([jnp.cos(angle), -jnp.sin(angle)], axis=1)
    back_angle = 2.0 * math.pi / 512.0 * (freqs[:, None] * freqs[None, :] % 512).astype(jnp.float32)
    inverse = jnp.concatenate([jnp.cos(back_angle), -jnp.sin(back_angle)], axis=0) / 512.0
    return (forward, inverse)


def convolve(field, profile, forward, inverse):
    widths, cells = field.shape
    blocks = cells // 256
    spectra = jnp.dot(
        field.reshape(widths * blocks, 256),
        forward,
        precision=lax.Precision.HIGHEST,
        preferred_element_type=jnp.float32,
    ).reshape(widths, blocks, 2, 512)
    kernel = jnp.dot(
        profile, forward, precision=lax.Precision.HIGHEST, preferred_element_type=jnp.float32
    ).reshape(widths, 1, 2, 512)
    real_part = jnp.sum(
        spectra[:, :, 0] * kernel[:, :, 0] - spectra[:, :, 1] * kernel[:, :, 1], axis=0
    )
    imag_part = jnp.sum(
        spectra[:, :, 0] * kernel[:, :, 1] + spectra[:, :, 1] * kernel[:, :, 0], axis=0
    )
    image = jnp.dot(
        jnp.concatenate([real_part, imag_part], axis=1),
        inverse,
        precision=lax.Precision.HIGHEST,
        preferred_element_type=jnp.float32,
    )
    zero_row = jnp.zeros((1, 256), jnp.float32)
    summed = jnp.concatenate([image[:, :256], zero_row], axis=0) + jnp.concatenate(
        [zero_row, image[:, 256:]], axis=0
    )
    return summed.reshape(-1)


def bin_lines(weight_low, weight_high, bin_row, low_cell):
    total = weight_low.size
    block_size = math.gcd(total, 2048)
    block_count = total // block_size
    row_count = NW * (G // 128)
    row_ids = jnp.arange(row_count, dtype=jnp.int32)
    column_ids = jnp.arange(256, dtype=jnp.int32)
    zero_value = jnp.zeros((), jnp.bfloat16)

    def deposit(totals, pieces):
        lower, upper, rows_here, cells_here = pieces
        hitting = (rows_here[None, :] == row_ids[:, None]).astype(jnp.bfloat16)
        placed = jnp.where(cells_here[:, None] == column_ids[None, :], lower[:, None], zero_value)
        placed = placed + jnp.where(
            cells_here[:, None] + 1 == column_ids[None, :], upper[:, None], zero_value
        )
        return (totals + jnp.dot(hitting, placed, preferred_element_type=jnp.float32), None)

    pieces = (
        weight_low.reshape(block_count, block_size),
        weight_high.reshape(block_count, block_size),
        bin_row.reshape(block_count, block_size),
        low_cell.reshape(block_count, block_size),
    )
    raw_sums, _ = lax.scan(deposit, jnp.zeros((row_count, 256), jnp.float32), pieces)
    raw_sums = raw_sums.reshape(NW, G // 128, 256)
    folded = raw_sums[:, :, :128] + jnp.pad(raw_sums[:, :-1, 128:], ((0, 0), (1, 0), (0, 0)))
    return folded.reshape(NW, G)


def body(
    natural_logged_absorbance,
    lower_state_level,
    subgrid_shift_ratio,
    local_grid_slot,
    broadening_class,
    tallies_per_shard,
    heat_levels,
    sum_over_states_ratio,
    shape_kernels,
):
    segments = lax.axis_size("seg")
    line_count = natural_logged_absorbance.shape[0]
    slot_count = 4 * line_count // segments
    my_segment = lax.axis_index("seg")
    sent_counts = lax.dynamic_index_in_dim(tallies_per_shard, my_segment, 0, keepdims=False)
    starts = jnp.cumsum(sent_counts) - sent_counts
    absolute_heat_level = heat_levels[0]
    factor = sum_over_states_ratio[0]
    columns = jnp.arange(slot_count, dtype=jnp.int32)
    is_live = columns[None, :] < sent_counts[:, None]
    carried = jnp.stack(
        [
            natural_logged_absorbance,
            lower_state_level,
            subgrid_shift_ratio,
            local_grid_slot.astype(jnp.float32),
            broadening_class.astype(jnp.float32),
        ]
    )
    padded = jnp.pad(carried, ((0, 0), (0, slot_count)))

    def take_window(begin):
        return lax.dynamic_slice_in_dim(padded, begin, slot_count, 1)

    windows = jnp.transpose(jax.vmap(take_window)(starts), (1, 0, 2))
    bin_sent = jnp.where(is_live, windows[4], float(NW))
    picked = jnp.concatenate([windows[:4], bin_sent[None]], axis=0)
    fields_in = lax.all_to_all(picked, "seg", split_axis=1, concat_axis=1, tiled=True)
    transition_absorbance = factor * jnp.exp(
        fields_in[0]
        - planck_hc_over_boltzmann
        * fields_in[1]
        * (1.0 / absolute_heat_level - 1.0 / baseline_heat_level)
    )
    weight_low = (transition_absorbance * (1.0 - fields_in[2])).astype(jnp.bfloat16)
    weight_high = (transition_absorbance * fields_in[2]).astype(jnp.bfloat16)
    cell_index = fields_in[3].astype(jnp.int32)
    bin_index = fields_in[4].astype(jnp.int32)
    bin_row = bin_index * (G // 128) + cell_index // 128
    low_cell = cell_index % 128
    weight_low, weight_high, bin_row, low_cell = (weight_low, weight_high, bin_row, low_cell)
    binned = bin_lines(
        weight_low.reshape(-1), weight_high.reshape(-1), bin_row.reshape(-1), low_cell.reshape(-1)
    )
    forward, inverse = dft_tables()
    profile = shape_kernels[0]
    margin = profile.shape[1] // 2
    widened = extended(binned, (("seg", 1),), margin)
    summed = convolve(widened, profile, forward, inverse)
    result = summed[2 * margin : 2 * margin + G]
    return result[None, :]


def solution(mesh):
    in_specs = (
        P("seg"),
        P("seg"),
        P("seg"),
        P("seg"),
        P("seg"),
        P(),
        P("tp"),
        P("tp"),
        P("tp", None, None),
    )
    out_specs = P("tp", "seg")
    return jax.shard_map(body, mesh=mesh, in_specs=in_specs, out_specs=out_specs, check_vma=False)
```

profile of v0, /device:TPU:1, one launch (start us, length us, event | category | flops | bytes accessed | tf_op | source)
XLA Modules:
  0.0 209.3 jit_solution(11021034554569526924)
XLA Ops:
  3.8 92.1 %while.14 = (s32[]{:T(128)}, f32[5,13056]{1,0:T(8,128)S(1)}, s32[64,2]{1,0:T(8,128)S(1)}, f32[64,5,768]{2,1,0:T(8,128)S(1)}, s32[]{:T(128)}) while((s32[]{:T(128)}, f32[5,13056]{1,0:T(8,128)S(1)}, s32[64,2]{1,0:T(8,128)S(1)}, f32[64,5,768]{2,1,0:T(8,128)S(1)}, s32[]{:T(128)}) %tuple.58), condition=%wide.while_cond, body=%wide.while_body.sunk | while | flops 2 | bytes 49249 | solution.py:137
  96.4 1.5 pad_maximum_fusion
  97.8 15.0 %all-to-all-start = ((f32[5,64,768]{2,0,1:T(8,128)}), f32[5,64,768]{2,0,1:T(8,128)}, u32[]{:S(2)}, u32[]{:S(2)}) async-start(f32[5,64,768]{2,0,1:T(8,128)} %pad_maximum_fusion), calls=%async_computation | async-start | bytes 3145728 | tf_op jit(solution)/shard_map/all_to_all | solution.py:142
  114.1 2.1 sine_negate_fusion.1
  117.3 5.3 %sine_negate_fusion = (f32[512,512]{1,0:T(8,128)S(1)}, f32[512,512]{1,0:T(8,128)}) fusion(), kind=kLoop, calls=%fused_computation.37 | loop fusion | flops 3932160 | bytes 2097152 | tf_op jit(solution)/shard_map/neg | solution.py:39
  123.3 29.3 %all-to-all-done = f32[5,64,768]{2,0,1:T(8,128)} async-done(((f32[5,64,768]{2,0,1:T(8,128)}), f32[5,64,768]{2,0,1:T(8,128)}, u32[]{:S(2)}, u32[]{:S(2)}) %all-to-all-start) | async-done | bytes 983072 | tf_op jit(solution)/shard_map/all_to_all | solution.py:142
  152.6 3.9 %slice_reduce_fusion = (f32[64,768]{1,0:T(8,128)S(1)}, f32[64,768]{1,0:T(8,128)S(1)}) fusion(f32[5,64,768]{2,0,1:T(8,128)} %all-to-all-done, f32[]{:T(128)} %bitcast.9, f32[]{:T(128)} %bitcast.68), kind=kLoop, calls=%fused_computation.64 | loop fusion | flops 147456 | bytes 983048 | tf_op jit(solution)/shard_map/slice | solution.py:149
  156.6 3.2 %fusion.36 = (s32[64,768]{1,0:T(8,128)S(1)}, s32[64,768]{1,0:T(8,128)S(1)}) fusion(f32[5,64,768]{2,0,1:T(8,128)} %all-to-all-done), kind=kLoop, calls=%fused_computation.68 | loop fusion | flops 147456 | bytes 786432 | tf_op jit(solution)/shard_map/convert_element_type | solution.py:151
  160.2 36.4 %while.15 = (s32[]{:T(128)}, f32[256,256]{1,0:T(8,128)S(1)}, s32[24,2048]{1,0:T(8,128)S(1)}, s32[24,2048]{1,0:T(8,128)S(1)}, bf16[24,2048]{1,0:T(8,128)(2,1)S(1)...) while((s32[]{:T(128)}, f32[256,256]{1,0:T(8,128)S(1)}, ...), condition=%wide.region_2.3_spmd.clone.clone, body=%wide.region_1.2_spmd.clone.clone.sunk | while | flops 273287168 | bytes 622695 | solution.py:98
  160.3 1.4 fusion.59
  161.8 1.4 fusion.59
  163.3 1.4 fusion.59
  164.8 1.4 fusion.59
  166.4 1.4 fusion.59
  167.9 1.4 fusion.59
  169.4 1.4 fusion.59
  172.4 1.4 fusion.59
  186.1 1.4 fusion.59
  189.1 1.4 fusion.59
  192.1 1.4 fusion.59
  195.2 1.4 fusion.59
  196.7 2.8 %collective-permute-start = (f32[16,128]{1,0:T(8,128)S(1)}, f32[16,128]{1,0:T(8,128)S(1)}, u32[]{:S(2)}, u32[]{:S(2)}) collective-permute-start(f32[16,128]{1,0:T(8,128)S(1)} %get-tuple-element.161), channel_id=1, source_target_pairs={{0,8},{8,16},{16,24},{24,32},{32,40},{40,48},{48,56},{56,64},{64,7... | collective-permute-start | bytes 24584 | tf_op jit(solution)/shard_map/ppermute | solution.py:24
  199.5 1.9 collective-permute-start.1
  201.6 2.9 %collective-permute-done.1 = f32[16,128]{1,0:T(8,128)S(1)} collective-permute-done((f32[16,128]{1,0:T(8,128)S(1)}, f32[16,128]{1,0:T(8,128)S(1)}, u32[]{:S(2)}, u32[]{:S(2)}) %collective-permute-start.1) | collective-permute-done | bytes 8224 | tf_op jit(solution)/shard_map/ppermute | solution.py:26
  (322 shorter events, 122.0 us)
Async XLA Ops:
  0.0 116.2 %copy-start = (f32[1,16,256]{2,1,0:T(8,128)S(1)}, f32[1,16,256]{2,1,0:T(8,128)}, u32[]{:S(2)}) copy-start(f32[1,16,256]{2,1,0:T(8,128)} %param.19) | copy-start | bytes 49156
  97.8 54.7 %all-to-all-start = ((f32[5,64,768]{2,0,1:T(8,128)}), f32[5,64,768]{2,0,1:T(8,128)}, u32[]{:S(2)}, u32[]{:S(2)}) async-start(f32[5,64,768]{2,0,1:T(8,128)} %pad_maximum_fusion), calls=%async_computation | async-start | bytes 3145728 | tf_op jit(solution)/shard_map/all_to_all | solution.py:142
  196.6 5.0 %copy-start.3 = (f32[16,1,1,512]{3,2,0,1:T(1,128)S(1)}, f32[16,1,1,512]{3,2,0,1:T(1,128)}, u32[]{:S(2)}) copy-start(f32[16,1,1,512]{3,2,0,1:T(1,128)} %get-tuple-element.164) | copy-start | bytes 98308
  196.6 5.0 %copy-start.2 = (f32[16,1,1,512]{3,2,0,1:T(1,128)S(1)}, f32[16,1,1,512]{3,2,0,1:T(1,128)}, u32[]{:S(2)}) copy-start(f32[16,1,1,512]{3,2,0,1:T(1,128)} %get-tuple-element.163) | copy-start | bytes 98308
  196.7 4.9 %collective-permute-start = (f32[16,128]{1,0:T(8,128)S(1)}, f32[16,128]{1,0:T(8,128)S(1)}, u32[]{:S(2)}, u32[]{:S(2)}) collective-permute-start(f32[16,128]{1,0:T(8,128)S(1)} %get-tuple-element.161), channel_id=1, source_target_pairs={{0,8},{8,16},{16,24},{24,32},{32,40},{40,48},{48,56},{56,64},{64,7... | collective-permute-start | bytes 24584 | tf_op jit(solution)/shard_map/ppermute | solution.py:24
  199.5 5.0 %collective-permute-start.1 = (f32[16,128]{1,0:T(8,128)S(1)}, f32[16,128]{1,0:T(8,128)S(1)}, u32[]{:S(2)}, u32[]{:S(2)}) collective-permute-start(f32[16,128]{1,0:T(8,128)S(1)} %get-tuple-element.162), channel_id=1, source_target_pairs={{8,0},{16,8},{24,16},{32,24},{40,32},{48,40},{56,48},{64,56},{72,6... | collective-permute-start | bytes 24584 | tf_op jit(solution)/shard_map/ppermute | solution.py:26
  201.6 6.0 %copy-start.1 = (f32[512,512]{1,0:T(8,128)S(1)}, f32[512,512]{1,0:T(8,128)}, u32[]{:S(2)}) copy-start(f32[512,512]{1,0:T(8,128)} %get-tuple-element.172) | copy-start | bytes 3145732
where the time goes:
time: 211 us; the launch traced here: 209 us
  local copies, waits for them, and re-layouts  98.8 us (47%)
  matrix products  36.5 us (17%)
  waiting for transfers between devices  32.2 us (15%)
  starting transfers between devices  19.8 us (9%)
  other arithmetic  19.2 us (9%)
    gather x192, local copies, waits for them, and re-layouts  91.9 us
    dot_general x24, matrix products, deposit(): jnp.dot(hitting, placed, preferred_element_type=jnp.float32)  33.1 us
    all_to_all x1, waiting for transfers between devices, body(): lax.all_to_all(picked, 'seg', split_axis=1, concat_axis=1, tiled=True)  29.3 us
    all_to_all x1, starting transfers between devices, body(): lax.all_to_all(picked, 'seg', split_axis=1, concat_axis=1, tiled=True)  15 us
    neg x1, other arithmetic, dft_tables(): -jnp.sin(back_angle)  5.29 us
  transfers between devices with their start and end apart: 3, of which 2 were waited for; matrix products, arithmetic and copies ran while one was open for 4% of the time, Pallas kernels for 0%

commit v1 on v0

v1 whole, which is shorter than its diff:
```python
import functools

import jax
import jax.numpy as jnp
from jax import lax
from jax.experimental import pallas as pl
from jax.experimental.pallas import tpu as pltpu
from jax.sharding import PartitionSpec as P

MESH = pl.DeviceIdType.MESH

G = 2048
NW = 16
POINTS = 8
CAP = 768
FIELDS = 5
J = 9
JW = 8 * NW
COLS = POINTS * JW + JW
BLOCKS = G // 8
PARTS = CAP // 128
SPAN = 384
REACH = 272
PACK = 4

planck_hc_over_boltzmann = 1.4388
baseline_heat_level = 900.0


def split(x):
    high = x.astype(jnp.bfloat16)
    return high, (x - high.astype(jnp.float32)).astype(jnp.bfloat16)


def kernel(
    n,
    heat_ref,
    ratio_ref,
    tallies_ref,
    absorb_ref,
    level_ref,
    shift_ref,
    slot_ref,
    class_ref,
    shape_ref,
    out_ref,
    heat,
    ratio,
    tallies,
    absorb,
    level,
    shift,
    slot,
    width,
    lines,
    starts,
    send,
    recv,
    points,
    shapes,
    rows0,
    cols0,
    rows1,
    cols1,
    acc,
    taps_high,
    taps_low,
    bins_high,
    bins_low,
    main_send,
    left_send,
    right_send,
    main_recv,
    left_recv,
    right_recv,
    ordered,
    in_sem,
    send_sem,
    first_sem,
    recv_sem,
    point_send_sem,
    point_sem,
    shape_send_sem,
    shape_sem,
    main_send_sem,
    main_sem,
    halo_send_sem,
    halo_sem,
):
    me = lax.axis_index("seg")
    tp = lax.axis_index("tp")
    left = lax.rem(me + n - 1, n)
    right = lax.rem(me + 1, n)

    eight = pl.multiple_of((me // 8) * 8, 8)
    copies = [
        pltpu.make_async_copy(src, dst, in_sem.at[k])
        for k, (src, dst) in enumerate(
            (
                (heat_ref, heat),
                (ratio_ref, ratio),
                (tallies_ref.at[pl.ds(eight, 8)], tallies),
                (absorb_ref, absorb),
                (level_ref, level),
                (shift_ref, shift),
                (slot_ref, slot),
                (class_ref, width),
                (shape_ref, shapes.at[0]),
            )
        )
    ]
    for copy in copies:
        copy.start()

    eighth = lax.rem(tp + n - lax.rem(me, 8), 8)
    stays = eighth == lax.rem(me, 8)
    octets = n // 8

    def partner(i):
        return eighth + 8 * lax.rem(me // 8 + i, octets)

    barrier = pltpu.get_barrier_semaphore()

    def greet(segment, point):
        pl.semaphore_signal(
            barrier, inc=1, device_id=(segment, point), device_id_type=MESH
        )

    for i in range(octets):
        if i == 0:
            pl.when(jnp.logical_not(stays))(lambda: greet(partner(0), tp))
        else:
            greet(partner(i), tp)
    for i in range(1, POINTS):
        for segment in (me, left, right):
            greet(segment, lax.rem(tp + i, POINTS))
    greet(left, tp)
    greet(right, tp)

    lane8 = lax.broadcasted_iota(jnp.int32, (8, 128), 1)
    sub8 = lax.broadcasted_iota(jnp.int32, (8, 128), 0)
    acc[...] = jnp.zeros_like(acc)

    for copy in copies[:3]:
        copy.wait()

    points[0] = jnp.where(lane8[:1] < 64, heat[0, 0], ratio[0, 0])

    def add_up(d, total):
        for u in range(8):
            starts[8 * d + u] = total
            total = total + tallies[lax.rem(me, 8), 8 * d + u]
        return total

    lax.fori_loop(0, octets, add_up, jnp.int32(0))

    for copy in copies[3:]:
        copy.wait()

    tiles = absorb.shape[0]
    lines[pl.ds(0, tiles), 0, :] = absorb[...]
    lines[pl.ds(0, tiles), 1, :] = level[...]
    lines[pl.ds(0, tiles), 2, :] = shift[...]
    lines[pl.ds(0, tiles), 3, :] = slot[...].astype(jnp.float32)
    lines[pl.ds(0, tiles), 4, :] = width[...].astype(jnp.float32)
    lines[pl.ds(tiles, 8)] = jnp.zeros((8, 8, 128), jnp.float32)

    def pack(target):
        begin = starts[target]
        count = tallies[lax.rem(me, 8), target]
        tile = lax.shift_right_logical(begin, 7)
        offset = jnp.full((8, 128), lax.bitwise_and(begin, 127))
        held = [lines[tile + q] for q in range(PARTS + 1)]
        windows = []
        for q in range(PARTS):
            window = jnp.where(lane8 >= offset, held[q], held[q + 1])
            for unit in (1, 4, 16):
                digit = lax.bitwise_and(offset, 3 * unit)
                turned = [pltpu.roll(window, 128 - k * unit, 1) for k in (1, 2, 3)]
                for k in (1, 2, 3):
                    window = jnp.where(digit == k * unit, turned[k - 1], window)
            turned = pltpu.roll(window, 64, 1)
            window = jnp.where(offset >= 64, turned, window)
            dead = jnp.logical_and(sub8 == 4, lane8 + 128 * q >= count)
            windows.append(jnp.where(dead, float(NW), window)[:FIELDS])
        return windows

    def pack_some(batch, _):
        first = batch * PACK
        packed = [pack(partner(first + u)) for u in range(PACK)]
        for u in range(PACK):
            for q in range(PARTS):
                send[first + u, q] = packed[u][q]
        return 0

    lax.fori_loop(0, octets // PACK, pack_some, 0)

    pl.semaphore_wait(barrier, octets + 2 + 3 * (POINTS - 1) - jnp.where(stays, 1, 0))

    def share(src, dst, sem_send, sem_recv):
        for i in range(1, POINTS):
            pltpu.make_async_remote_copy(
                src_ref=src.at[0],
                dst_ref=dst.at[i],
                send_sem=sem_send,
                recv_sem=sem_recv,
                device_id=(me, lax.rem(tp + i, POINTS)),
                device_id_type=MESH,
            ).start()

    def lines_to(i, sem):
        return pltpu.make_async_remote_copy(
            src_ref=send.at[i],
            dst_ref=recv.at[i],
            send_sem=sem,
            recv_sem=recv_sem.at[i],
            device_id=(partner(i), tp),
            device_id_type=MESH,
        )

    pl.when(jnp.logical_not(stays))(lambda: lines_to(0, first_sem).start())
    pl.when(stays)(
        lambda: pltpu.make_async_copy(
            send.at[0], recv.at[0], recv_sem.at[0]
        ).start()
    )
    share(points, points, point_send_sem, point_sem)
    for i in range(1, octets):
        lines_to(i, send_sem).start()
    share(shapes, shapes, shape_send_sem, shape_sem)

    def all_points(src, dst, sem_send, sem_recv):
        return pltpu.make_async_remote_copy(
            src_ref=src.at[pl.ds(1, POINTS - 1)],
            dst_ref=dst.at[pl.ds(1, POINTS - 1)],
            send_sem=sem_send,
            recv_sem=sem_recv,
            device_id=(me, lax.rem(tp + 1, POINTS)),
            device_id_type=MESH,
        )

    all_points(points, points, point_send_sem, point_sem).wait_recv()
    both = jnp.concatenate([points[i] for i in range(POINTS)], axis=0)
    heats = jnp.where(lane8 < 64, both, pltpu.roll(both, 64, 1))
    ratios = jnp.where(lane8 < 64, pltpu.roll(both, 64, 1), both)
    inverse_gap = 1.0 / heats - 1.0 / baseline_heat_level

    block_ids = lax.broadcasted_iota(jnp.int32, (128, BLOCKS), 1).astype(jnp.float32)
    width_ids = lax.broadcasted_iota(jnp.int32, (NW, 128), 0).astype(jnp.float32)
    width_row = lax.broadcasted_iota(jnp.int32, (JW, SPAN), 0)

    def spread(row):
        return jnp.broadcast_to(row, (NW, 128)).astype(jnp.bfloat16)

    def arrived(g):
        pltpu.make_async_remote_copy(
            src_ref=send.at[g],
            dst_ref=recv.at[g],
            send_sem=send_sem,
            recv_sem=recv_sem.at[g],
            device_id=(partner(1), tp),
            device_id_type=MESH,
        ).wait_recv()

    def one_hots(g, rows, cols):
        slots = [recv[g, part, 3:4, :] for part in range(PARTS)]
        slots = jnp.concatenate(slots + [slots[0]] * (8 - PARTS), axis=0)
        blocks = jnp.floor(slots * 0.125)
        cells = slots - 8.0 * blocks
        tall = blocks.T
        return [
            functools.partial(one_hot, g, part, cells[part : part + 1], tall, rows, cols)
            for part in range(PARTS)
        ]

    def one_hot(g, part, cell, tall, rows, cols):
        piece = recv[g, part]
        at = part * 128
        hits = jnp.broadcast_to(tall[:, part : part + 1], (128, BLOCKS)) == block_ids
        rows[pl.ds(at, 128), :] = jnp.where(hits, 1.0, 0.0).astype(jnp.bfloat16)
        strength = ratios * jnp.exp(
            piece[0:1] - planck_hc_over_boltzmann * piece[1:2] * inverse_gap
        )
        low = strength * (1.0 - piece[2:3])
        high = strength * piece[2:3]
        half_cell = cell * 0.5
        is_even = jnp.broadcast_to(half_cell == jnp.floor(half_cell), (POINTS, 128))
        evens = jnp.where(is_even, low, high)
        odds = jnp.where(is_even, high, low)
        is_width = jnp.broadcast_to(piece[4:5], (NW, 128)) == width_ids
        is_width = jnp.where(is_width, 1.0, 0.0).astype(jnp.bfloat16)
        here = [cell == float(j) for j in range(8)]
        touched = [
            here[0],
            *(jnp.logical_or(here[j], here[j - 1]) for j in range(1, 8)),
            here[7],
        ]
        touched = [spread(jnp.where(t, 1.0, 0.0)) for t in touched]
        for p in range(POINTS):
            even = spread(evens[p : p + 1]) * is_width
            odd = spread(odds[p : p + 1]) * is_width
            for j in range(J):
                top = p * JW + j * NW if j < 8 else POINTS * JW + p * NW
                value = (odd if j % 2 else even) * touched[j]
                cols[pl.ds(top, NW), pl.ds(at, 128)] = value

    def add_product(piece, rows, cols):
        some = pl.ds(piece * (COLS // PARTS), COLS // PARTS)
        acc[some] += jnp.dot(
            cols[some], rows[...], preferred_element_type=jnp.float32
        )

    def make_taps(p):
        taps = jnp.concatenate([shapes[p], jnp.zeros((NW, 128), jnp.float32)], axis=1)
        moved = [taps] + [pltpu.roll(taps, j, 1) for j in range(1, J)]
        ninth = jnp.concatenate([moved[8]] * POINTS, axis=0)
        ninth = jnp.where(width_row // NW == p, ninth, 0.0)
        every = jnp.concatenate(moved[:8] + [ninth], axis=0)
        high, low = split(every.T[:REACH])
        taps_high[p] = high
        taps_low[p] = low

    def step(g, rows, cols, last_rows, last_cols):
        arrived(g)
        for part, make in enumerate(one_hots(g, rows, cols)):
            make()
            add_product(part, last_rows, last_cols)
        make_taps(g)

    arrived(0)
    for make in one_hots(0, rows0, cols0):
        make()
    all_points(shapes, shapes, shape_send_sem, shape_sem).wait_recv()

    def deposit(h, _):
        step(2 * h + 1, rows1, cols1, rows0, cols0)
        step(2 * h + 2, rows0, cols0, rows1, cols1)
        return 0

    lax.fori_loop(0, octets // 2 - 1, deposit, 0)
    step(octets - 1, rows1, cols1, rows0, cols0)
    make_taps(0)
    for piece in range(PARTS):
        add_product(piece, rows1, cols1)
    high, low = split(acc[...])
    bins_high[...] = high
    bins_low[...] = low

    def fold(x):
        kept = jnp.where(lane8 < 16, x, 0.0)
        moved = pltpu.roll(kept, 0, 1, stride=16, stride_axis=0)
        return jnp.sum(moved, axis=0, keepdims=True)

    def unfold(row):
        wide = jnp.broadcast_to(row, (8, 128))
        moved = wide
        for i in range(1, 8):
            moved = jnp.where(sub8 == i, pltpu.roll(wide, 128 - 16 * i, 1), moved)
        return jnp.where(lane8 < 16, moved, 0.0)

    def convolve(p):
        own = pl.ds(pl.multiple_of(p * JW, JW), JW)
        ninth = pl.ds(POINTS * JW, JW)
        bin_high = jnp.concatenate([bins_high[own], bins_high[ninth]], axis=0)
        bin_low = jnp.concatenate([bins_low[own], bins_low[ninth]], axis=0)
        product = jnp.dot(taps_high[p], bin_high, preferred_element_type=jnp.float32)
        product += jnp.dot(taps_low[p], bin_high, preferred_element_type=jnp.float32)
        product += jnp.dot(taps_high[p], bin_low, preferred_element_type=jnp.float32)
        first, second = product[128:136, :128], product[128:136, 128:]
        outside = jnp.zeros((8, 128), jnp.float32)
        for m in range(33):
            by = m - 16
            if by == 0:
                continue
            front, back = product[8 * m : 8 * m + 8, :128], product[8 * m : 8 * m + 8, 128:]
            front = pltpu.roll(front, by % 128, 1)
            back = pltpu.roll(back, by % 128, 1)
            if by > 0:
                wraps = lane8 < by
                first += jnp.where(wraps, 0.0, front)
                second += jnp.where(wraps, front, back)
                outside += jnp.where(wraps, back, 0.0)
            else:
                wraps = lane8 >= 128 + by
                first += jnp.where(wraps, back, front)
                second += jnp.where(wraps, 0.0, back)
                outside += jnp.where(wraps, front, 0.0)
        main_send[p, 0] = first
        main_send[p, 1] = second
        left_send[p] = fold(pltpu.roll(outside, 16, 1))
        right_send[p] = fold(outside)

    def send_sums(p):
        point = lax.rem(tp + POINTS - p, POINTS)

        @pl.when(p > 0)
        def _():
            pltpu.make_async_remote_copy(
                src_ref=main_send.at[p],
                dst_ref=main_recv.at[p],
                send_sem=main_send_sem,
                recv_sem=main_sem,
                device_id=(me, point),
                device_id_type=MESH,
            ).start()

        for k, (src, dst, segment) in enumerate(
            ((left_send, left_recv, left), (right_send, right_recv, right))
        ):
            pltpu.make_async_remote_copy(
                src_ref=src.at[p],
                dst_ref=dst.at[p],
                send_sem=halo_send_sem.at[k],
                recv_sem=halo_sem.at[k],
                device_id=(segment, point),
                device_id_type=MESH,
            ).start()

    def convolve_two(h, _):
        pair = (POINTS // 2 + h, POINTS // 2 - 1 - h)
        for p in pair:
            convolve(p)
        for p in pair:
            send_sums(p)
        return 0

    lax.fori_loop(0, POINTS // 2, convolve_two, 0)

    sums = all_points(main_send, main_recv, main_send_sem, main_sem)
    halos = [
        pltpu.make_async_remote_copy(
            src_ref=src,
            dst_ref=dst,
            send_sem=halo_send_sem.at[k],
            recv_sem=halo_sem.at[k],
            device_id=(segment, tp),
            device_id_type=MESH,
        )
        for k, (src, dst, segment) in enumerate(
            ((left_send, left_recv, left), (right_send, right_recv, right))
        )
    ]
    for halo in halos:
        halo.wait_recv()
    from_right = unfold(jnp.sum(left_recv[...], axis=0))
    from_left = unfold(jnp.sum(right_recv[...], axis=0))
    from_right = jnp.where(me < n - 1, pltpu.roll(from_right, 112, 1), 0.0)
    from_left = jnp.where(me > 0, from_left, 0.0)
    first = main_send[0, 0] + from_left
    second = main_send[0, 1] + from_right
    sums.wait_recv()
    for p in range(1, POINTS):
        first += main_recv[p, 0]
        second += main_recv[p, 1]
    for k, part in enumerate((first, second)):
        tall = jnp.concatenate([part, jnp.zeros((120, 128), jnp.float32)], axis=0)
        ordered[pl.ds(128 * k, 128), :] = tall.T
    total = ordered[pl.ds(0, 16, stride=16), :]
    for k in range(1, 16):
        total += pltpu.roll(ordered[pl.ds(k, 16, stride=16), :], 8 * k, 1)
    out_ref[...] = total

    all_points(points, points, point_send_sem, point_sem).wait_send()
    all_points(shapes, shapes, shape_send_sem, shape_sem).wait_send()
    pl.when(jnp.logical_not(stays))(lambda: lines_to(0, first_sem).wait_send())
    pltpu.make_async_remote_copy(
        src_ref=send.at[pl.ds(1, octets - 1)],
        dst_ref=recv.at[pl.ds(1, octets - 1)],
        send_sem=send_sem,
        recv_sem=recv_sem.at[1],
        device_id=(partner(1), tp),
        device_id_type=MESH,
    ).wait_send()
    sums.wait_send()
    for halo in halos:
        halo.wait_send()


def body(
    natural_logged_absorbance,
    lower_state_level,
    subgrid_shift_ratio,
    local_grid_slot,
    broadening_class,
    tallies_per_shard,
    heat_levels,
    sum_over_states_ratio,
    shape_kernels,
):
    n = lax.axis_size("seg")
    lines = natural_logged_absorbance.shape[0]
    tiles = lines // 128
    hbm = pl.BlockSpec(memory_space=pl.ANY)
    vmem = pl.BlockSpec(memory_space=pltpu.VMEM)
    f32, bf16, i32 = jnp.float32, jnp.bfloat16, jnp.int32
    dma = pltpu.SemaphoreType.DMA
    result = pl.pallas_call(
        functools.partial(kernel, n),
        out_shape=jax.ShapeDtypeStruct((16, 128), f32),
        in_specs=[hbm] * 9,
        out_specs=vmem,
        scratch_shapes=[
            pltpu.SMEM((1, 1), f32),
            pltpu.SMEM((1, 1), f32),
            pltpu.SMEM((8, n), i32),
            pltpu.VMEM((tiles, 128), f32),
            pltpu.VMEM((tiles, 128), f32),
            pltpu.VMEM((tiles, 128), f32),
            pltpu.VMEM((tiles, 128), i32),
            pltpu.VMEM((tiles, 128), i32),
            pltpu.VMEM((tiles + 8, 8, 128), f32),
            pltpu.SMEM((n,), i32),
            pltpu.VMEM((n // 8, PARTS, FIELDS, 128), f32),
            pltpu.VMEM((n // 8, PARTS, FIELDS, 128), f32),
            pltpu.VMEM((POINTS, 1, 128), f32),
            pltpu.VMEM((POINTS, NW, 256), f32),
            pltpu.VMEM((CAP, BLOCKS), bf16),
            pltpu.VMEM((COLS, CAP), bf16),
            pltpu.VMEM((CAP, BLOCKS), bf16),
            pltpu.VMEM((COLS, CAP), bf16),
            pltpu.VMEM((COLS, BLOCKS), f32),
            pltpu.VMEM((POINTS, REACH, 2 * JW), bf16),
            pltpu.VMEM((POINTS, REACH, 2 * JW), bf16),
            pltpu.VMEM((COLS, BLOCKS), bf16),
            pltpu.VMEM((COLS, BLOCKS), bf16),
            pltpu.VMEM((POINTS, 2, 8, 128), f32),
            pltpu.VMEM((POINTS, 1, 128), f32),
            pltpu.VMEM((POINTS, 1, 128), f32),
            pltpu.VMEM((POINTS, 2, 8, 128), f32),
            pltpu.VMEM((POINTS, 1, 128), f32),
            pltpu.VMEM((POINTS, 1, 128), f32),
            pltpu.VMEM((BLOCKS, 128), f32),
            dma((9,)),
            dma,
            dma,
            dma((n // 8,)),
            dma,
            dma,
            dma,
            dma,
            dma,
            dma,
            dma((2,)),
            dma((2,)),
        ],
        compiler_params=pltpu.CompilerParams(
            collective_id=0, has_side_effects=True, vmem_limit_bytes=56541184
        ),
        cost_estimate=pl.CostEstimate(
            flops=2 * n * CAP // 8 * BLOCKS * COLS,
            bytes_accessed=300000,
            transcendentals=n * CAP // 8 * POINTS,
        ),
    )(
        heat_levels.reshape(1, 1),
        sum_over_states_ratio.reshape(1, 1),
        tallies_per_shard,
        natural_logged_absorbance.reshape(tiles, 128),
        lower_state_level.reshape(tiles, 128),
        subgrid_shift_ratio.reshape(tiles, 128),
        local_grid_slot.reshape(tiles, 128),
        broadening_class.reshape(tiles, 128),
        shape_kernels[0],
    )
    return result.reshape(1, G)


def solution(mesh):
    in_specs = (
        P("seg"),
        P("seg"),
        P("seg"),
        P("seg"),
        P("seg"),
        P(),
        P("tp"),
        P("tp"),
        P("tp", None, None),
    )
    out_specs = P("tp", "seg")
    return jax.shard_map(body, mesh=mesh, in_specs=in_specs, out_specs=out_specs, check_vma=False)
```

time: 211 us -> 37.2 us (0.18)
  local copies, waits for them, and re-layouts: 98.8 us -> 0.6 us
  matrix products: 36.5 us -> 0 us
  Pallas kernels: 0 us -> 35.2 us
  waiting for transfers between devices: 32.2 us -> 0 us
  starting transfers between devices: 19.8 us -> 0 us
  other arithmetic: 19.2 us -> 0 us
    gather x192 -> x0, local copies, waits for them, and re-layouts: 91.9 us -> none
    dot_general x27 -> x0, matrix products: 36.5 us -> none  [the longest x24 33.1 us: deposit(): jnp.dot(hitting, placed, preferred_element_type=jnp.float32)]
    pallas_call x0 -> x1, Pallas kernels: none -> 35.2 us  [body(): pl.pallas_call(functools.partial(kernel, n), out_shape=jax.ShapeDtypeStru...]
    all_to_all x1 -> x0, waiting for transfers between devices: 29.3 us -> none  [body(): lax.all_to_all(picked, 'seg', split_axis=1, concat_axis=1, tiled=True)]
    all_to_all x1 -> x0, starting transfers between devices: 15 us -> none  [body(): lax.all_to_all(picked, 'seg', split_axis=1, concat_axis=1, tiled=True)]
    neg x2 -> x0, other arithmetic: 7.36 us -> none  [the longest x1 5.29 us: dft_tables(): -jnp.sin(back_angle)]
    convert_element_type x4 -> x0, other arithmetic: 4.84 us -> none  [the longest x1 3.2 us: body(): cell_index = fields_in[3].astype(jnp.int32)]
    ppermute x2 -> x0, starting transfers between devices: 4.77 us -> none  [the longest x1 2.85 us: extended(): lax.ppermute(tail, axis, [(i, (i + 1) % count) for i in range(ends)])]
  transfers between devices with their start and end apart: 3 -> 0, of which waited for: 2 -> 0; matrix products, arithmetic and copies ran while one was open for 4% -> 0% of each run, Pallas kernels for 0% -> 0%
where the time goes in v1:
time: 37.2 us; the launch traced here: 37.1 us
  Pallas kernels  35.2 us (95%)
  between operations  1.3 us (3%)
  local copies, waits for them, and re-layouts  0.6 us (2%)
    pallas_call x1, Pallas kernels, body(): pl.pallas_call(functools.partial(kernel, n), out_shape=jax.ShapeDtypeStru...  35.2 us

profile of v1, /device:TPU:1, one launch (start us, length us, event | category | flops | bytes accessed | tf_op | source)
XLA Modules:
  0.0 37.1 jit_solution(6453467858191909439)
XLA Ops:
  1.3 35.2 %shard_map.91 = f32[16,128]{1,0:T(8,128)S(1)} custom-call(f32[1,1]{1,0:T(1,128)} %bitcast.9.heat_ref, f32[1,1]{1,0:T(1,128)} %bitcast.10.ratio_ref, s32[64,64]{1,0:T(8,128)} %tallies_ref.1, f32[96,128]{1,0:T(8,128)} %bitcast.12, f32[96,128]{1,0:T(8,128)} %bitcast.13, f32[96,128]{1,0:T(8,128)} %bitcast.14, s32[96,128]{1,0:T(8,128)} %bitcast.15, ...), custom_call_target="tpu_custom_call" | custom-call | flops 3623878656 | bytes 300000 | tf_op jit(solution)/shard_map/pallas_call | solution.py:497
  36.5 0.6 %copy.13 = f32[1,2048]{1,0:T(1,128)} copy(f32[1,2048]{1,0:T(1,128)S(1)} %bitcast.11) | data formatting | bytes 16384

commit v2 on v1

--- a/solution.py
+++ b/solution.py
@@ -52,7 +52,8 @@
     shift,
     slot,
     width,
-    lines,
+    slot_value,
+    width_value,
     starts,
     send,
     recv,
@@ -92,6 +93,7 @@
     left = lax.rem(me + n - 1, n)
     right = lax.rem(me + 1, n)
 
+    tiles = slot.shape[0]
     eight = pl.multiple_of((me // 8) * 8, 8)
     copies = [
         pltpu.make_async_copy(src, dst, in_sem.at[k])
@@ -100,9 +102,9 @@
                 (heat_ref, heat),
                 (ratio_ref, ratio),
                 (tallies_ref.at[pl.ds(eight, 8)], tallies),
-                (absorb_ref, absorb),
-                (level_ref, level),
-                (shift_ref, shift),
+                (absorb_ref, absorb.at[pl.ds(0, tiles)]),
+                (level_ref, level.at[pl.ds(0, tiles)]),
+                (shift_ref, shift.at[pl.ds(0, tiles)]),
                 (slot_ref, slot),
                 (class_ref, width),
                 (shape_ref, shapes.at[0]),
@@ -157,23 +159,22 @@
     for copy in copies[3:]:
         copy.wait()
 
-    tiles = absorb.shape[0]
-    lines[pl.ds(0, tiles), 0, :] = absorb[...]
-    lines[pl.ds(0, tiles), 1, :] = level[...]
-    lines[pl.ds(0, tiles), 2, :] = shift[...]
-    lines[pl.ds(0, tiles), 3, :] = slot[...].astype(jnp.float32)
-    lines[pl.ds(0, tiles), 4, :] = width[...].astype(jnp.float32)
-    lines[pl.ds(tiles, 8)] = jnp.zeros((8, 8, 128), jnp.float32)
+    fields = (absorb, level, shift, slot_value, width_value)
+    slot_value[pl.ds(0, tiles)] = slot[...].astype(jnp.float32)
+    width_value[pl.ds(0, tiles)] = width[...].astype(jnp.float32)
+    for field in fields:
+        field[pl.ds(tiles, 16)] = jnp.zeros((16, 128), jnp.float32)
+    position = 128 * sub8 + lane8
 
     def pack(target):
         begin = starts[target]
         count = tallies[lax.rem(me, 8), target]
         tile = lax.shift_right_logical(begin, 7)
         offset = jnp.full((8, 128), lax.bitwise_and(begin, 127))
-        held = [lines[tile + q] for q in range(PARTS + 1)]
+        here, after = pl.ds(tile, 8), pl.ds(tile + 1, 8)
         windows = []
-        for q in range(PARTS):
-            window = jnp.where(lane8 >= offset, held[q], held[q + 1])
+        for f, field in enumerate(fields):
+            window = jnp.where(lane8 >= offset, field[here, :], field[after, :])
             for unit in (1, 4, 16):
                 digit = lax.bitwise_and(offset, 3 * unit)
                 turned = [pltpu.roll(window, 128 - k * unit, 1) for k in (1, 2, 3)]
@@ -181,16 +182,17 @@
                     window = jnp.where(digit == k * unit, turned[k - 1], window)
             turned = pltpu.roll(window, 64, 1)
             window = jnp.where(offset >= 64, turned, window)
-            dead = jnp.logical_and(sub8 == 4, lane8 + 128 * q >= count)
-            windows.append(jnp.where(dead, float(NW), window)[:FIELDS])
+            if f == FIELDS - 1:
+                window = jnp.where(position >= count, float(NW), window)
+            windows.append(window[:PARTS])
         return windows
 
     def pack_some(batch, _):
         first = batch * PACK
         packed = [pack(partner(first + u)) for u in range(PACK)]
         for u in range(PACK):
-            for q in range(PARTS):
-                send[first + u, q] = packed[u][q]
+            for f in range(FIELDS):
+                send[first + u, f] = packed[u][f]
         return 0
 
     lax.fori_loop(0, octets // PACK, pack_some, 0)
@@ -263,46 +265,45 @@
         ).wait_recv()
 
     def one_hots(g, rows, cols):
-        slots = [recv[g, part, 3:4, :] for part in range(PARTS)]
-        slots = jnp.concatenate(slots + [slots[0]] * (8 - PARTS), axis=0)
+        absorbs, levels, shifts, slots, widths = (recv[g, f] for f in range(FIELDS))
         blocks = jnp.floor(slots * 0.125)
         cells = slots - 8.0 * blocks
-        tall = blocks.T
-        return [
-            functools.partial(one_hot, g, part, cells[part : part + 1], tall, rows, cols)
-            for part in range(PARTS)
-        ]
-
-    def one_hot(g, part, cell, tall, rows, cols):
-        piece = recv[g, part]
-        at = part * 128
-        hits = jnp.broadcast_to(tall[:, part : part + 1], (128, BLOCKS)) == block_ids
-        rows[pl.ds(at, 128), :] = jnp.where(hits, 1.0, 0.0).astype(jnp.bfloat16)
-        strength = ratios * jnp.exp(
-            piece[0:1] - planck_hc_over_boltzmann * piece[1:2] * inverse_gap
-        )
-        low = strength * (1.0 - piece[2:3])
-        high = strength * piece[2:3]
-        half_cell = cell * 0.5
-        is_even = jnp.broadcast_to(half_cell == jnp.floor(half_cell), (POINTS, 128))
-        evens = jnp.where(is_even, low, high)
-        odds = jnp.where(is_even, high, low)
-        is_width = jnp.broadcast_to(piece[4:5], (NW, 128)) == width_ids
-        is_width = jnp.where(is_width, 1.0, 0.0).astype(jnp.bfloat16)
-        here = [cell == float(j) for j in range(8)]
+        halves = cells * 0.5
+        even_cell = jnp.where(halves == jnp.floor(halves), 1.0, 0.0)
+        here = [cells == float(j) for j in range(8)]
         touched = [
             here[0],
             *(jnp.logical_or(here[j], here[j - 1]) for j in range(1, 8)),
             here[7],
         ]
-        touched = [spread(jnp.where(t, 1.0, 0.0)) for t in touched]
-        for p in range(POINTS):
-            even = spread(evens[p : p + 1]) * is_width
-            odd = spread(odds[p : p + 1]) * is_width
-            for j in range(J):
-                top = p * JW + j * NW if j < 8 else POINTS * JW + p * NW
-                value = (odd if j % 2 else even) * touched[j]
-                cols[pl.ds(top, NW), pl.ds(at, 128)] = value
+        touched = [jnp.where(t, 1.0, 0.0) for t in touched]
+        tall = jnp.concatenate([blocks, blocks[: 8 - PARTS]], axis=0).T
+        scaled = planck_hc_over_boltzmann * levels
+        below = 1.0 - shifts
+
+        def one_hot(part):
+            line = slice(part, part + 1)
+            at = part * 128
+            hits = jnp.broadcast_to(tall[:, line], (128, BLOCKS)) == block_ids
+            rows[pl.ds(at, 128), :] = jnp.where(hits, 1.0, 0.0).astype(jnp.bfloat16)
+            strength = ratios * jnp.exp(absorbs[line] - scaled[line] * inverse_gap)
+            low = strength * below[line]
+            high = strength * shifts[line]
+            is_even = jnp.broadcast_to(even_cell[line], (POINTS, 128)) > 0.5
+            evens = jnp.where(is_even, low, high)
+            odds = jnp.where(is_even, high, low)
+            is_width = jnp.broadcast_to(widths[line], (NW, 128)) == width_ids
+            is_width = jnp.where(is_width, 1.0, 0.0).astype(jnp.bfloat16)
+            cell_hits = [spread(t[line]) for t in touched]
+            for p in range(POINTS):
+                even = spread(evens[p : p + 1]) * is_width
+                odd = spread(odds[p : p + 1]) * is_width
+                for j in range(J):
+                    top = p * JW + j * NW if j < 8 else POINTS * JW + p * NW
+                    value = (odd if j % 2 else even) * cell_hits[j]
+                    cols[pl.ds(top, NW), pl.ds(at, 128)] = value
+
+        return [functools.partial(one_hot, part) for part in range(PARTS)]
 
     def add_product(piece, rows, cols):
         some = pl.ds(piece * (COLS // PARTS), COLS // PARTS)
@@ -503,15 +504,16 @@
             pltpu.SMEM((1, 1), f32),
             pltpu.SMEM((1, 1), f32),
             pltpu.SMEM((8, n), i32),
-            pltpu.VMEM((tiles, 128), f32),
-            pltpu.VMEM((tiles, 128), f32),
-            pltpu.VMEM((tiles, 128), f32),
+            pltpu.VMEM((tiles + 16, 128), f32),
+            pltpu.VMEM((tiles + 16, 128), f32),
+            pltpu.VMEM((tiles + 16, 128), f32),
             pltpu.VMEM((tiles, 128), i32),
             pltpu.VMEM((tiles, 128), i32),
-            pltpu.VMEM((tiles + 8, 8, 128), f32),
+            pltpu.VMEM((tiles + 16, 128), f32),
+            pltpu.VMEM((tiles + 16, 128), f32),
             pltpu.SMEM((n,), i32),
-            pltpu.VMEM((n // 8, PARTS, FIELDS, 128), f32),
-            pltpu.VMEM((n // 8, PARTS, FIELDS, 128), f32),
+            pltpu.VMEM((n // 8, FIELDS, PARTS, 128), f32),
+            pltpu.VMEM((n // 8, FIELDS, PARTS, 128), f32),
             pltpu.VMEM((POINTS, 1, 128), f32),
             pltpu.VMEM((POINTS, NW, 256), f32),
             pltpu.VMEM((CAP, BLOCKS), bf16),

time: 37.2 us -> 37 us (level)
  no operation moved by 1% of the time
where the time goes in v2:
time: 37 us; the launch traced here: 36.8 us
  Pallas kernels  34.9 us (94%)
  between operations  1.3 us (4%)
  local copies, waits for them, and re-layouts  0.6 us (2%)
    pallas_call x1, Pallas kernels, body(): pl.pallas_call(functools.partial(kernel, n), out_shape=jax.ShapeDtypeStru...  34.9 us

profile of v2, /device:TPU:1, one launch (start us, length us, event | category | flops | bytes accessed | tf_op | source)
XLA Modules:
  0.0 36.8 jit_solution(9121542045184449935)
XLA Ops:
  1.3 34.9 %shard_map.91 = f32[16,128]{1,0:T(8,128)S(1)} custom-call(f32[1,1]{1,0:T(1,128)} %bitcast.9.heat_ref, f32[1,1]{1,0:T(1,128)} %bitcast.10.ratio_ref, s32[64,64]{1,0:T(8,128)} %tallies_ref.1, f32[96,128]{1,0:T(8,128)} %bitcast.12, f32[96,128]{1,0:T(8,128)} %bitcast.13, f32[96,128]{1,0:T(8,128)} %bitcast.14, s32[96,128]{1,0:T(8,128)} %bitcast.15, ...), custom_call_target="tpu_custom_call" | custom-call | flops 3623878656 | bytes 300000 | tf_op jit(solution)/shard_map/pallas_call | solution.py:498
  36.2 0.6 %copy.13 = f32[1,2048]{1,0:T(1,128)} copy(f32[1,2048]{1,0:T(1,128)S(1)} %bitcast.11) | data formatting | bytes 16384

commit v3 on v2

--- a/solution.py
+++ b/solution.py
@@ -19,7 +19,6 @@
 COLS = POINTS * JW + JW
 BLOCKS = G // 8
 PARTS = CAP // 128
-SPAN = 384
 REACH = 272
 PACK = 4
 
@@ -249,7 +248,7 @@
 
     block_ids = lax.broadcasted_iota(jnp.int32, (128, BLOCKS), 1).astype(jnp.float32)
     width_ids = lax.broadcasted_iota(jnp.int32, (NW, 128), 0).astype(jnp.float32)
-    width_row = lax.broadcasted_iota(jnp.int32, (JW, SPAN), 0)
+    point_lane = lax.broadcasted_iota(jnp.int32, (REACH, JW), 1) // NW
 
     def spread(row):
         return jnp.broadcast_to(row, (NW, 128)).astype(jnp.bfloat16)
@@ -313,11 +312,11 @@
 
     def make_taps(p):
         taps = jnp.concatenate([shapes[p], jnp.zeros((NW, 128), jnp.float32)], axis=1)
-        moved = [taps] + [pltpu.roll(taps, j, 1) for j in range(1, J)]
-        ninth = jnp.concatenate([moved[8]] * POINTS, axis=0)
-        ninth = jnp.where(width_row // NW == p, ninth, 0.0)
-        every = jnp.concatenate(moved[:8] + [ninth], axis=0)
-        high, low = split(every.T[:REACH])
+        moved = [taps] + [pltpu.roll(taps, j, 1) for j in range(1, 8)]
+        tall = jnp.concatenate(moved, axis=0).T[:REACH]
+        ninth = jnp.concatenate([jnp.zeros((8, JW), jnp.float32), tall[:-8]], axis=0)
+        ninth = jnp.where(point_lane == p, pltpu.roll(ninth, NW * p, 1), 0.0)
+        high, low = split(jnp.concatenate([tall, ninth], axis=1))
         taps_high[p] = high
         taps_low[p] = low
 
@@ -328,6 +327,7 @@
             add_product(part, last_rows, last_cols)
         make_taps(g)
 
+    make_taps(0)
     arrived(0)
     for make in one_hots(0, rows0, cols0):
         make()
@@ -340,7 +340,6 @@
 
     lax.fori_loop(0, octets // 2 - 1, deposit, 0)
     step(octets - 1, rows1, cols1, rows0, cols0)
-    make_taps(0)
     for piece in range(PARTS):
         add_product(piece, rows1, cols1)
     high, low = split(acc[...])

time: 37 us -> 36.9 us (level)
  no operation moved by 1% of the time
where the time goes in v3:
time: 36.9 us; the launch traced here: 36.7 us
  Pallas kernels  34.8 us (94%)
  between operations  1.3 us (4%)
  local copies, waits for them, and re-layouts  0.6 us (2%)
    pallas_call x1, Pallas kernels, body(): pl.pallas_call(functools.partial(kernel, n), out_shape=jax.ShapeDtypeStru...  34.8 us

profile of v3, /device:TPU:1, one launch (start us, length us, event | category | flops | bytes accessed | tf_op | source)
XLA Modules:
  0.0 36.7 jit_solution(12947956924632159052)
XLA Ops:
  1.3 34.8 %shard_map.91 = f32[16,128]{1,0:T(8,128)S(1)} custom-call(f32[1,1]{1,0:T(1,128)} %bitcast.9.heat_ref, f32[1,1]{1,0:T(1,128)} %bitcast.10.ratio_ref, s32[64,64]{1,0:T(8,128)} %tallies_ref.1, f32[96,128]{1,0:T(8,128)} %bitcast.12, f32[96,128]{1,0:T(8,128)} %bitcast.13, f32[96,128]{1,0:T(8,128)} %bitcast.14, s32[96,128]{1,0:T(8,128)} %bitcast.15, ...), custom_call_target="tpu_custom_call" | custom-call | flops 3623878656 | bytes 300000 | tf_op jit(solution)/shard_map/pallas_call | solution.py:497
  36.1 0.6 %copy.13 = f32[1,2048]{1,0:T(1,128)} copy(f32[1,2048]{1,0:T(1,128)S(1)} %bitcast.11) | data formatting | bytes 16384

commit v4 on v3

--- a/solution.py
+++ b/solution.py
@@ -58,6 +58,8 @@
     recv,
     points,
     shapes,
+    hits,
+    weights,
     rows0,
     cols0,
     rows1,
@@ -264,39 +266,45 @@
         ).wait_recv()
 
     def one_hots(g, rows, cols):
-        absorbs, levels, shifts, slots, widths = (recv[g, f] for f in range(FIELDS))
-        blocks = jnp.floor(slots * 0.125)
-        cells = slots - 8.0 * blocks
+        blocks = jnp.floor(recv[g, 3] * 0.125)
+        cells = recv[g, 3] - 8.0 * blocks
         halves = cells * 0.5
-        even_cell = jnp.where(halves == jnp.floor(halves), 1.0, 0.0)
         here = [cells == float(j) for j in range(8)]
         touched = [
             here[0],
             *(jnp.logical_or(here[j], here[j - 1]) for j in range(1, 8)),
             here[7],
+            halves == jnp.floor(halves),
         ]
-        touched = [jnp.where(t, 1.0, 0.0) for t in touched]
+        for j, hit in enumerate(touched):
+            hits[j, pl.ds(0, PARTS)] = jnp.where(hit, 1.0, 0.0)
         tall = jnp.concatenate([blocks, blocks[: 8 - PARTS]], axis=0).T
-        scaled = planck_hc_over_boltzmann * levels
-        below = 1.0 - shifts
 
         def one_hot(part):
-            line = slice(part, part + 1)
+            line = pl.ds(part, 1)
             at = part * 128
-            hits = jnp.broadcast_to(tall[:, line], (128, BLOCKS)) == block_ids
-            rows[pl.ds(at, 128), :] = jnp.where(hits, 1.0, 0.0).astype(jnp.bfloat16)
-            strength = ratios * jnp.exp(absorbs[line] - scaled[line] * inverse_gap)
-            low = strength * below[line]
-            high = strength * shifts[line]
-            is_even = jnp.broadcast_to(even_cell[line], (POINTS, 128)) > 0.5
-            evens = jnp.where(is_even, low, high)
-            odds = jnp.where(is_even, high, low)
-            is_width = jnp.broadcast_to(widths[line], (NW, 128)) == width_ids
-            is_width = jnp.where(is_width, 1.0, 0.0).astype(jnp.bfloat16)
-            cell_hits = [spread(t[line]) for t in touched]
+
+            def field(f, height):
+                return jnp.broadcast_to(recv[g, f, line, :], (height, 128))
+
+            in_block = jnp.broadcast_to(tall[:, part : part + 1], (128, BLOCKS)) == block_ids
+            rows[pl.ds(at, 128), :] = jnp.where(in_block, 1.0, 0.0).astype(jnp.bfloat16)
+            strength = ratios * jnp.exp(
+                field(0, POINTS)
+                - planck_hc_over_boltzmann * field(1, POINTS) * inverse_gap
+            )
+            low = strength * (1.0 - field(2, POINTS))
+            high = strength * field(2, POINTS)
+            is_even = jnp.broadcast_to(hits[J, line, :], (POINTS, 128)) > 0.5
+            weights[part, 0] = jnp.where(is_even, low, high)
+            weights[part, 1] = jnp.where(is_even, high, low)
+            is_width = jnp.where(field(4, NW) == width_ids, 1.0, 0.0)
+            is_width = is_width.astype(jnp.bfloat16)
+            cell_hits = [spread(hits[j, line, :]) for j in range(J)]
             for p in range(POINTS):
-                even = spread(evens[p : p + 1]) * is_width
-                odd = spread(odds[p : p + 1]) * is_width
+                even, odd = (
+                    spread(weights[part, k, pl.ds(p, 1), :]) * is_width for k in range(2)
+                )
                 for j in range(J):
                     top = p * JW + j * NW if j < 8 else POINTS * JW + p * NW
                     value = (odd if j % 2 else even) * cell_hits[j]
@@ -515,6 +523,8 @@
             pltpu.VMEM((n // 8, FIELDS, PARTS, 128), f32),
             pltpu.VMEM((POINTS, 1, 128), f32),
             pltpu.VMEM((POINTS, NW, 256), f32),
+            pltpu.VMEM((J + 1, 8, 128), f32),
+            pltpu.VMEM((PARTS, 2, POINTS, 128), f32),
             pltpu.VMEM((CAP, BLOCKS), bf16),
             pltpu.VMEM((COLS, CAP), bf16),
             pltpu.VMEM((CAP, BLOCKS), bf16),

time: 36.9 us -> 37.1 us (level)
  no operation moved by 1% of the time
where the time goes in v4:
time: 37.1 us; the launch traced here: 37 us
  Pallas kernels  35 us (94%)
  between operations  1.3 us (4%)
  local copies, waits for them, and re-layouts  0.6 us (2%)
    pallas_call x1, Pallas kernels, body(): pl.pallas_call(functools.partial(kernel, n), out_shape=jax.ShapeDtypeStru...  35 us

profile of v4, /device:TPU:1, one launch (start us, length us, event | category | flops | bytes accessed | tf_op | source)
XLA Modules:
  0.0 37.0 jit_solution(10451666729215176059)
XLA Ops:
  1.3 35.0 %shard_map.91 = f32[16,128]{1,0:T(8,128)S(1)} custom-call(f32[1,1]{1,0:T(1,128)} %bitcast.9.heat_ref, f32[1,1]{1,0:T(1,128)} %bitcast.10.ratio_ref, s32[64,64]{1,0:T(8,128)} %tallies_ref.1, f32[96,128]{1,0:T(8,128)} %bitcast.12, f32[96,128]{1,0:T(8,128)} %bitcast.13, f32[96,128]{1,0:T(8,128)} %bitcast.14, s32[96,128]{1,0:T(8,128)} %bitcast.15, ...), custom_call_target="tpu_custom_call" | custom-call | flops 3623878656 | bytes 300000 | tf_op jit(solution)/shard_map/pallas_call | solution.py:505
  36.3 0.6 %copy.13 = f32[1,2048]{1,0:T(1,128)} copy(f32[1,2048]{1,0:T(1,128)S(1)} %bitcast.11) | data formatting | bytes 16384

commit v5 on v3

--- a/solution.py
+++ b/solution.py
@@ -304,11 +304,17 @@
 
         return [functools.partial(one_hot, part) for part in range(PARTS)]
 
+    def rows_of(piece):
+        return pl.ds(piece * (COLS // PARTS), COLS // PARTS)
+
+    def added(piece, rows, cols):
+        some = rows_of(piece)
+        return acc[some] + jnp.dot(
+            cols[some], rows[...], preferred_element_type=jnp.float32
+        )
+
     def add_product(piece, rows, cols):
-        some = pl.ds(piece * (COLS // PARTS), COLS // PARTS)
-        acc[some] += jnp.dot(
-            cols[some], rows[...], preferred_element_type=jnp.float32
-        )
+        acc[rows_of(piece)] = added(piece, rows, cols)
 
     def make_taps(p):
         taps = jnp.concatenate([shapes[p], jnp.zeros((NW, 128), jnp.float32)], axis=1)
@@ -341,10 +347,9 @@
     lax.fori_loop(0, octets // 2 - 1, deposit, 0)
     step(octets - 1, rows1, cols1, rows0, cols0)
     for piece in range(PARTS):
-        add_product(piece, rows1, cols1)
-    high, low = split(acc[...])
-    bins_high[...] = high
-    bins_low[...] = low
+        high, low = split(added(piece, rows1, cols1))
+        bins_high[rows_of(piece)] = high
+        bins_low[rows_of(piece)] = low
 
     def fold(x):
         kept = jnp.where(lane8 < 16, x, 0.0)
@@ -393,8 +398,7 @@
     def send_sums(p):
         point = lax.rem(tp + POINTS - p, POINTS)
 
-        @pl.when(p > 0)
-        def _():
+        if p > 0:
             pltpu.make_async_remote_copy(
                 src_ref=main_send.at[p],
                 dst_ref=main_recv.at[p],
@@ -416,15 +420,15 @@
                 device_id_type=MESH,
             ).start()
 
-    def convolve_two(h, _):
-        pair = (POINTS // 2 + h, POINTS // 2 - 1 - h)
+    pairs = [(POINTS // 2 + h, POINTS // 2 - 1 - h) for h in range(POINTS // 2)]
+    for h, pair in enumerate(pairs):
         for p in pair:
             convolve(p)
-        for p in pair:
-            send_sums(p)
-        return 0
-
-    lax.fori_loop(0, POINTS // 2, convolve_two, 0)
+        if h > 0:
+            for p in pairs[h - 1]:
+                send_sums(p)
+    for p in pairs[-1]:
+        send_sums(p)
 
     sums = all_points(main_send, main_recv, main_send_sem, main_sem)
     halos = [

time: 36.9 us -> 37.1 us (level)
  no operation moved by 1% of the time
where the time goes in v5:
time: 37.1 us; the launch traced here: 36.9 us
  Pallas kernels  35 us (94%)
  between operations  1.3 us (4%)
  local copies, waits for them, and re-layouts  0.6 us (2%)
    pallas_call x1, Pallas kernels, body(): pl.pallas_call(functools.partial(kernel, n), out_shape=jax.ShapeDtypeStru...  35 us

profile of v5, /device:TPU:1, one launch (start us, length us, event | category | flops | bytes accessed | tf_op | source)
XLA Modules:
  0.0 36.9 jit_solution(13620497254953833755)
XLA Ops:
  1.3 35.0 %shard_map.91 = f32[16,128]{1,0:T(8,128)S(1)} custom-call(f32[1,1]{1,0:T(1,128)} %bitcast.9.heat_ref, f32[1,1]{1,0:T(1,128)} %bitcast.10.ratio_ref, s32[64,64]{1,0:T(8,128)} %tallies_ref.1, f32[96,128]{1,0:T(8,128)} %bitcast.12, f32[96,128]{1,0:T(8,128)} %bitcast.13, f32[96,128]{1,0:T(8,128)} %bitcast.14, s32[96,128]{1,0:T(8,128)} %bitcast.15, ...), custom_call_target="tpu_custom_call" | custom-call | flops 3623878656 | bytes 300000 | tf_op jit(solution)/shard_map/pallas_call | solution.py:501
  36.3 0.6 %copy.13 = f32[1,2048]{1,0:T(1,128)} copy(f32[1,2048]{1,0:T(1,128)S(1)} %bitcast.11) | data formatting | bytes 16384

commit v6 on v3

--- a/solution.py
+++ b/solution.py
@@ -321,10 +321,9 @@
         taps_low[p] = low
 
     def step(g, rows, cols, last_rows, last_cols):
-        arrived(g)
         for part, make in enumerate(one_hots(g, rows, cols)):
+            add_product(part, last_rows, last_cols)
             make()
-            add_product(part, last_rows, last_cols)
         make_taps(g)
 
     make_taps(0)
@@ -334,11 +333,14 @@
     all_points(shapes, shapes, shape_send_sem, shape_sem).wait_recv()
 
     def deposit(h, _):
+        arrived(2 * h + 1)
+        arrived(2 * h + 2)
         step(2 * h + 1, rows1, cols1, rows0, cols0)
         step(2 * h + 2, rows0, cols0, rows1, cols1)
         return 0
 
     lax.fori_loop(0, octets // 2 - 1, deposit, 0)
+    arrived(octets - 1)
     step(octets - 1, rows1, cols1, rows0, cols0)
     for piece in range(PARTS):
         add_product(piece, rows1, cols1)

time: 36.9 us -> 36.7 us (level)
  no operation moved by 1% of the time
where the time goes in v6:
time: 36.7 us; the launch traced here: 36.5 us
  Pallas kernels  34.6 us (94%)
  between operations  1.3 us (4%)
  local copies, waits for them, and re-layouts  0.6 us (2%)
    pallas_call x1, Pallas kernels, body(): pl.pallas_call(functools.partial(kernel, n), out_shape=jax.ShapeDtypeStru...  34.6 us

profile of v6, /device:TPU:1, one launch (start us, length us, event | category | flops | bytes accessed | tf_op | source)
XLA Modules:
  0.0 36.5 jit_solution(1038869670964211429)
XLA Ops:
  1.3 34.6 %shard_map.91 = f32[16,128]{1,0:T(8,128)S(1)} custom-call(f32[1,1]{1,0:T(1,128)} %bitcast.9.heat_ref, f32[1,1]{1,0:T(1,128)} %bitcast.10.ratio_ref, s32[64,64]{1,0:T(8,128)} %tallies_ref.1, f32[96,128]{1,0:T(8,128)} %bitcast.12, f32[96,128]{1,0:T(8,128)} %bitcast.13, f32[96,128]{1,0:T(8,128)} %bitcast.14, s32[96,128]{1,0:T(8,128)} %bitcast.15, ...), custom_call_target="tpu_custom_call" | custom-call | flops 3623878656 | bytes 300000 | tf_op jit(solution)/shard_map/pallas_call | solution.py:499
  35.9 0.6 %copy.13 = f32[1,2048]{1,0:T(1,128)} copy(f32[1,2048]{1,0:T(1,128)S(1)} %bitcast.11) | data formatting | bytes 16384

commit v7 on v6

--- a/solution.py
+++ b/solution.py
@@ -324,24 +324,31 @@
         for part, make in enumerate(one_hots(g, rows, cols)):
             add_product(part, last_rows, last_cols)
             make()
-        make_taps(g)
 
     make_taps(0)
     arrived(0)
     for make in one_hots(0, rows0, cols0):
         make()
+    arrived(1)
+    arrived(2)
+    step(1, rows1, cols1, rows0, cols0)
+    step(2, rows0, cols0, rows1, cols1)
     all_points(shapes, shapes, shape_send_sem, shape_sem).wait_recv()
 
     def deposit(h, _):
         arrived(2 * h + 1)
         arrived(2 * h + 2)
         step(2 * h + 1, rows1, cols1, rows0, cols0)
+        make_taps(3 * h - 2)
         step(2 * h + 2, rows0, cols0, rows1, cols1)
+        make_taps(3 * h - 1)
+        make_taps(3 * h)
         return 0
 
-    lax.fori_loop(0, octets // 2 - 1, deposit, 0)
+    lax.fori_loop(1, octets // 2 - 1, deposit, 0)
     arrived(octets - 1)
     step(octets - 1, rows1, cols1, rows0, cols0)
+    make_taps(octets - 1)
     for piece in range(PARTS):
         add_product(piece, rows1, cols1)
     high, low = split(acc[...])

time: 36.7 us -> 36.1 us (0.984)
  Pallas kernels: 34.6 us -> 34 us
    pallas_call x1, Pallas kernels: 34.6 us -> 34 us  [body(): pl.pallas_call(functools.partial(kernel, n), out_shape=jax.ShapeDtypeStru...]
where the time goes in v7:
time: 36.1 us; the launch traced here: 35.9 us
  Pallas kernels  34 us (94%)
  between operations  1.3 us (4%)
  local copies, waits for them, and re-layouts  0.6 us (2%)
    pallas_call x1, Pallas kernels, body(): pl.pallas_call(functools.partial(kernel, n), out_shape=jax.ShapeDtypeStru...  34 us

profile of v7, /device:TPU:1, one launch (start us, length us, event | category | flops | bytes accessed | tf_op | source)
XLA Modules:
  0.0 35.9 jit_solution(5033270868172613740)
XLA Ops:
  1.3 34.0 %shard_map.91 = f32[16,128]{1,0:T(8,128)S(1)} custom-call(f32[1,1]{1,0:T(1,128)} %bitcast.9.heat_ref, f32[1,1]{1,0:T(1,128)} %bitcast.10.ratio_ref, s32[64,64]{1,0:T(8,128)} %tallies_ref.1, f32[96,128]{1,0:T(8,128)} %bitcast.12, f32[96,128]{1,0:T(8,128)} %bitcast.13, f32[96,128]{1,0:T(8,128)} %bitcast.14, s32[96,128]{1,0:T(8,128)} %bitcast.15, ...), custom_call_target="tpu_custom_call" | custom-call | flops 3623878656 | bytes 300000 | tf_op jit(solution)/shard_map/pallas_call | solution.py:506
  35.3 0.6 %copy.13 = f32[1,2048]{1,0:T(1,128)} copy(f32[1,2048]{1,0:T(1,128)S(1)} %bitcast.11) | data formatting | bytes 16384

commit v8 on v6

--- a/solution.py
+++ b/solution.py
@@ -324,13 +324,11 @@
         for part, make in enumerate(one_hots(g, rows, cols)):
             add_product(part, last_rows, last_cols)
             make()
-        make_taps(g)
 
     make_taps(0)
     arrived(0)
     for make in one_hots(0, rows0, cols0):
         make()
-    all_points(shapes, shapes, shape_send_sem, shape_sem).wait_recv()
 
     def deposit(h, _):
         arrived(2 * h + 1)
@@ -339,9 +337,19 @@
         step(2 * h + 2, rows0, cols0, rows1, cols1)
         return 0
 
-    lax.fori_loop(0, octets // 2 - 1, deposit, 0)
-    arrived(octets - 1)
+    lax.fori_loop(0, octets // 2 - 2, deposit, 0)
+    all_points(shapes, shapes, shape_send_sem, shape_sem).wait_recv()
+    for g in range(octets - 3, octets):
+        arrived(g)
+    step(octets - 3, rows1, cols1, rows0, cols0)
+    make_taps(1)
+    make_taps(2)
+    step(octets - 2, rows0, cols0, rows1, cols1)
+    make_taps(3)
+    make_taps(4)
     step(octets - 1, rows1, cols1, rows0, cols0)
+    for p in range(5, POINTS):
+        make_taps(p)
     for piece in range(PARTS):
         add_product(piece, rows1, cols1)
     high, low = split(acc[...])

time: 36.7 us -> 36.1 us (0.984)
  Pallas kernels: 34.6 us -> 34 us
    pallas_call x1, Pallas kernels: 34.6 us -> 34 us  [body(): pl.pallas_call(functools.partial(kernel, n), out_shape=jax.ShapeDtypeStru...]
where the time goes in v8:
time: 36.1 us; the launch traced here: 36 us
  Pallas kernels  34 us (94%)
  between operations  1.3 us (4%)
  local copies, waits for them, and re-layouts  0.6 us (2%)
    pallas_call x1, Pallas kernels, body(): pl.pallas_call(functools.partial(kernel, n), out_shape=jax.ShapeDtypeStru...  34 us

profile of v8, /device:TPU:1, one launch (start us, length us, event | category | flops | bytes accessed | tf_op | source)
XLA Modules:
  0.0 36.0 jit_solution(4363978322835833972)
XLA Ops:
  1.3 34.0 %shard_map.91 = f32[16,128]{1,0:T(8,128)S(1)} custom-call(f32[1,1]{1,0:T(1,128)} %bitcast.9.heat_ref, f32[1,1]{1,0:T(1,128)} %bitcast.10.ratio_ref, s32[64,64]{1,0:T(8,128)} %tallies_ref.1, f32[96,128]{1,0:T(8,128)} %bitcast.12, f32[96,128]{1,0:T(8,128)} %bitcast.13, f32[96,128]{1,0:T(8,128)} %bitcast.14, s32[96,128]{1,0:T(8,128)} %bitcast.15, ...), custom_call_target="tpu_custom_call" | custom-call | flops 3623878656 | bytes 300000 | tf_op jit(solution)/shard_map/pallas_call | solution.py:507
  35.4 0.6 %copy.13 = f32[1,2048]{1,0:T(1,128)} copy(f32[1,2048]{1,0:T(1,128)S(1)} %bitcast.11) | data formatting | bytes 16384

commit v9 on v8

--- a/solution.py
+++ b/solution.py
@@ -304,11 +304,17 @@
 
         return [functools.partial(one_hot, part) for part in range(PARTS)]
 
+    def rows_of(piece):
+        return pl.ds(piece * (COLS // PARTS), COLS // PARTS)
+
+    def added(piece, rows, cols):
+        some = rows_of(piece)
+        return acc[some] + jnp.dot(
+            cols[some], rows[...], preferred_element_type=jnp.float32
+        )
+
     def add_product(piece, rows, cols):
-        some = pl.ds(piece * (COLS // PARTS), COLS // PARTS)
-        acc[some] += jnp.dot(
-            cols[some], rows[...], preferred_element_type=jnp.float32
-        )
+        acc[rows_of(piece)] = added(piece, rows, cols)
 
     def make_taps(p):
         taps = jnp.concatenate([shapes[p], jnp.zeros((NW, 128), jnp.float32)], axis=1)
@@ -332,8 +338,8 @@
 
     def deposit(h, _):
         arrived(2 * h + 1)
+        step(2 * h + 1, rows1, cols1, rows0, cols0)
         arrived(2 * h + 2)
-        step(2 * h + 1, rows1, cols1, rows0, cols0)
         step(2 * h + 2, rows0, cols0, rows1, cols1)
         return 0
 
@@ -351,10 +357,9 @@
     for p in range(5, POINTS):
         make_taps(p)
     for piece in range(PARTS):
-        add_product(piece, rows1, cols1)
-    high, low = split(acc[...])
-    bins_high[...] = high
-    bins_low[...] = low
+        high, low = split(added(piece, rows1, cols1))
+        bins_high[rows_of(piece)] = high
+        bins_low[rows_of(piece)] = low
 
     def fold(x):
         kept = jnp.where(lane8 < 16, x, 0.0)

time: 36.1 us -> 36.6 us (1.014)
  Pallas kernels: 34 us -> 34.5 us
    pallas_call x1, Pallas kernels: 34 us -> 34.5 us  [body(): pl.pallas_call(functools.partial(kernel, n), out_shape=jax.ShapeDtypeStru...]
where the time goes in v9:
time: 36.6 us; the launch traced here: 36.4 us
  Pallas kernels  34.5 us (94%)
  between operations  1.3 us (4%)
  local copies, waits for them, and re-layouts  0.6 us (2%)
    pallas_call x1, Pallas kernels, body(): pl.pallas_call(functools.partial(kernel, n), out_shape=jax.ShapeDtypeStru...  34.5 us

profile of v9, /device:TPU:1, one launch (start us, length us, event | category | flops | bytes accessed | tf_op | source)
XLA Modules:
  0.0 36.4 jit_solution(18090791756124425930)
XLA Ops:
  1.3 34.5 %shard_map.91 = f32[16,128]{1,0:T(8,128)S(1)} custom-call(f32[1,1]{1,0:T(1,128)} %bitcast.9.heat_ref, f32[1,1]{1,0:T(1,128)} %bitcast.10.ratio_ref, s32[64,64]{1,0:T(8,128)} %tallies_ref.1, f32[96,128]{1,0:T(8,128)} %bitcast.12, f32[96,128]{1,0:T(8,128)} %bitcast.13, f32[96,128]{1,0:T(8,128)} %bitcast.14, s32[96,128]{1,0:T(8,128)} %bitcast.15, ...), custom_call_target="tpu_custom_call" | custom-call | flops 3623878656 | bytes 300000 | tf_op jit(solution)/shard_map/pallas_call | solution.py:512
  35.8 0.6 %copy.13 = f32[1,2048]{1,0:T(1,128)} copy(f32[1,2048]{1,0:T(1,128)S(1)} %bitcast.11) | data formatting | bytes 16384

commit v10 on v9

--- a/solution.py
+++ b/solution.py
@@ -338,8 +338,8 @@
 
     def deposit(h, _):
         arrived(2 * h + 1)
+        arrived(2 * h + 2)
         step(2 * h + 1, rows1, cols1, rows0, cols0)
-        arrived(2 * h + 2)
         step(2 * h + 2, rows0, cols0, rows1, cols1)
         return 0
 

time: 36.6 us -> 36.1 us (0.986)
  Pallas kernels: 34.5 us -> 34.1 us
    pallas_call x1, Pallas kernels: 34.5 us -> 34.1 us  [body(): pl.pallas_call(functools.partial(kernel, n), out_shape=jax.ShapeDtypeStru...]
where the time goes in v10:
time: 36.1 us; the launch traced here: 36 us
  Pallas kernels  34.1 us (94%)
  between operations  1.3 us (4%)
  local copies, waits for them, and re-layouts  0.6 us (2%)
    pallas_call x1, Pallas kernels, body(): pl.pallas_call(functools.partial(kernel, n), out_shape=jax.ShapeDtypeStru...  34.1 us

profile of v10, /device:TPU:1, one launch (start us, length us, event | category | flops | bytes accessed | tf_op | source)
XLA Modules:
  0.0 36.0 jit_solution(17537628210987299575)
XLA Ops:
  1.3 34.1 %shard_map.91 = f32[16,128]{1,0:T(8,128)S(1)} custom-call(f32[1,1]{1,0:T(1,128)} %bitcast.9.heat_ref, f32[1,1]{1,0:T(1,128)} %bitcast.10.ratio_ref, s32[64,64]{1,0:T(8,128)} %tallies_ref.1, f32[96,128]{1,0:T(8,128)} %bitcast.12, f32[96,128]{1,0:T(8,128)} %bitcast.13, f32[96,128]{1,0:T(8,128)} %bitcast.14, s32[96,128]{1,0:T(8,128)} %bitcast.15, ...), custom_call_target="tpu_custom_call" | custom-call | flops 3623878656 | bytes 300000 | tf_op jit(solution)/shard_map/pallas_call | solution.py:512
  35.4 0.6 %copy.13 = f32[1,2048]{1,0:T(1,128)} copy(f32[1,2048]{1,0:T(1,128)S(1)} %bitcast.11) | data formatting | bytes 16384
